TPU v7x, 128 devices: a whole 4x4x4 slice. The times are simulated.
128 devices in a mesh: cache: 16 (over z, y), seq: 8 (over x, core).
Axes of the slice: x: 4, y: 4, z: 4, core: 2. Of those that a mesh axis runs over, the one named last changes fastest.
Arguments:
- kv_store: bfloat16 [128, 512, 1024], P('cache', 'seq'), may hold values from -6 to 6
- span_slot: int32 [128], replicated, may hold values from 0 to 127, as said below
- retrieval: int32 [16, 8], P('cache'), may hold values from 0 to 127, as said below
- recompute: int32 [16, 8, 77], P('cache'), may hold values from 0 to 511, as said below
- fresh_kv: bfloat16 [16, 8, 77, 1024], P('cache'), may hold values from -6 to 6
- queries: bfloat16 [16, 1536, 4096], P('cache', 'seq'), may hold values from -128 to 128
- question_kv: bfloat16 [16, 1536, 1024], P('cache', 'seq'), may hold values from -6 to 6
Outputs:
- attended: bfloat16 [16, 1536, 4096], P('cache', 'seq')
Inputs may be any that keep to these rules, and one draw needn't show every extreme that they name: `span_slot`: a permutation: each slot holds exactly one span id; owner o holds slots o * 8 to (o + 1) * 8 - 1. `retrieval`: the ids of one request are distinct; at most 2 of them lie in one owner's slots, and in every request some owner holds exactly 2. `recompute`: the positions of one span of one request are distinct.
All inputs are finite; a program needn't handle non-finite values.
Results may differ from a plain program's by a relative error of at most 0.003.
Values may be sent and summed in bfloat16 or wider, within the bound.
A program may use at most 192 MiB of HBM per device.

v0:
```python
import jax
import jax.numpy as jnp
from jax import lax
from jax.sharding import PartitionSpec as P

HD = 128
KVH = 4
GROUP = 8


masked_score = -1e30


def block_scores(query_block, key_block, visible):
    scores = jnp.einsum(
        "qhd,kd->qhk", query_block, key_block, preferred_element_type=jnp.float32
    ) * HD ** (-0.5)
    return jnp.where(visible[:, None, :], scores, masked_score)


def query_blocks(query_rows):
    return query_rows.reshape(query_rows.shape[0], KVH * 2, GROUP // 2, HD).transpose(1, 0, 2, 3)


def head_slices(key_rows, group_id):
    key_width = KVH * HD
    key_block = lax.dynamic_slice_in_dim(key_rows, group_id * HD, HD, 1)
    value_block = lax.dynamic_slice_in_dim(key_rows, key_width + group_id * HD, HD, 1)
    return (key_block, value_block)


def attend_rows(query_rows, query_place, key_rows, key_place):
    visible = key_place[None, :] <= query_place[:, None]

    def one_block(block_args):
        block_index, query_block = block_args
        key_block, value_block = head_slices(key_rows, block_index // 2)
        scores = block_scores(query_block, key_block, visible)
        peak = jnp.max(scores, axis=-1, keepdims=True)
        weights = jnp.exp(scores - peak)
        totals = jnp.sum(weights, axis=-1)
        rounded = weights.astype(jnp.bfloat16)
        result = (
            jnp.einsum("qhk,kd->qhd", rounded, value_block, preferred_element_type=jnp.float32)
            / totals[..., None]
        )
        return result.astype(jnp.bfloat16)

    block_count = KVH * 2
    attended = lax.map(
        one_block, (jnp.arange(block_count, dtype=jnp.int32), query_blocks(query_rows))
    )
    return attended.transpose(1, 0, 2, 3).reshape(query_rows.shape[0], -1)


def on_device(kv_store, span_slot, retrieval, recompute, fresh_kv, queries, question_kv):
    slice_rows = kv_store.shape[1]
    features = kv_store.shape[2]
    seq_index = lax.axis_index("seq")
    own_slots = span_slot[retrieval[0]]
    gathered = lax.all_gather(kv_store, "cache", axis=0, tiled=True)
    cached = gathered[own_slots]
    token_place = seq_index * slice_rows + jnp.arange(slice_rows, dtype=jnp.int32)
    replace_mask = recompute[0][:, None, :] == token_place[None, :, None]
    fresh_rows = jnp.einsum(
        "jtm,jmf->jtf",
        replace_mask.astype(jnp.bfloat16),
        fresh_kv[0],
        preferred_element_type=jnp.float32,
    ).astype(jnp.bfloat16)
    context = jnp.where(jnp.any(replace_mask, axis=-1)[..., None], fresh_rows, cached)
    own_queries = queries[0]
    own_question = question_kv[0]
    query_count = own_queries.shape[0]
    query_place = seq_index * query_count + jnp.arange(query_count, dtype=jnp.int32)
    full_context, full_question = (
        lax.all_gather(context, "seq", axis=1, tiled=True),
        lax.all_gather(own_question, "seq", axis=0, tiled=True),
    )
    context_count = full_context.shape[0] * full_context.shape[1]
    key_rows = jnp.concatenate(
        [full_context.reshape(context_count, features), full_question], axis=0
    )
    key_place = jnp.concatenate(
        [
            jnp.full((context_count,), -1, dtype=jnp.int32),
            jnp.arange(full_question.shape[0], dtype=jnp.int32),
        ]
    )
    attended = attend_rows(own_queries, query_place, key_rows, key_place)
    return attended[None]


def solution(mesh):
    in_specs = (
        P("cache", "seq", None),
        P(),
        P("cache", None),
        P("cache", None, None),
        P("cache", None, None, None),
        P("cache", "seq", None),
        P("cache", "seq", None),
    )
    out_specs = P("cache", "seq", None)
    return jax.shard_map(
        on_device, mesh=mesh, in_specs=in_specs, out_specs=out_specs, check_vma=False
    )
```

profile of v0, /device:TPU:1, one launch (start us, length us, event | category | flops | bytes accessed | tf_op | source)
XLA Modules:
  0.0 491.9 jit_solution(16762010845721607376)
XLA Ops:
  6.5 0.7 all-gather.5.cloned.1.call-update
  7.3 0.7 all-gather.9.cloned.1.call-update
  8.1 0.7 fusion.42
  8.7 1.3 gather_fusion
  10.1 1.0 compare_reduce_fusion
  11.0 113.2 %all-gather.5.cloned.1.call-done = bf16[128,64,1024]{2,1,0:T(8,128)(2,1)} async-done(((bf16[8,64,1024]{2,1,0:T(8,128)(2,1)}), bf16[128,64,1024]{2,1,0:T(8,128)(2,1)}) %all-gather.5.cloned.1.call-update) | async-done | bytes 16777232 | tf_op jit(solution)/shard_map/all_gather | solution.py:61
  124.2 6.4 %gather_fusion.1 = bf16[8,64,1024]{2,1,0:T(8,128)(2,1)S(1)} fusion(bf16[128,64,1024]{2,1,0:T(8,128)(2,1)} %all-gather.5.cloned.1.call-done, s32[1024]{0:T(1024)S(1)} %pad_clamp_fusion), kind=kCustom, calls=%fused_computation.1 | custom fusion | bytes 2097184 | tf_op jit(solution)/shard_map/gather | solution.py:62
  130.6 3.3 fusion.37
  133.9 2.9 reshape_squeeze.3
  136.8 16.9 %all-gather.9.cloned.1.call-done = bf16[1,1536,1024]{2,1,0:T(8,128)(2,1)} async-done(((bf16[1,192,1024]{2,1,0:T(8,128)(2,1)}), bf16[1,1536,1024]{2,1,0:T(8,128)(2,1)}) %all-gather.9.cloned.1.call-update) | async-done | bytes 3145744 | tf_op jit(solution)/shard_map/all_gather | solution.py:78
  153.7 51.5 %all-gather.7.cloned.1.call-done = bf16[8,512,1024]{2,1,0:T(8,128)(2,1)} async-done(((bf16[8,64,1024]{2,1,0:T(8,128)(2,1)}), bf16[8,512,1024]{2,1,0:T(8,128)(2,1)}) %all-gather.7.cloned.1.call-update) | async-done | bytes 8388624 | tf_op jit(solution)/shard_map/all_gather | solution.py:77
  205.1 13.7 %pad_maximum_fusion = bf16[5632,1024]{1,0:T(8,128)(2,1)} fusion(bf16[1536,1024]{1,0:T(8,128)(2,1)} %bitcast.53, bf16[4096,1024]{1,0:T(8,128)(2,1)} %bitcast.51), kind=kLoop, calls=%fused_computation.26 | loop fusion | flops 23068672 | bytes 23068672 | tf_op jit(solution)/shard_map/concatenate | solution.py:81
  218.8 261.4 %while.13 = (s32[]{:T(128)}, bf16[8,192,4,128]{3,1,2,0:T(8,128)(2,1)}, bf16[8,192,4,128]{3,2,0,1:T(4,128)(2,1)S(1)}, s32[8]{0:T(128)S(1)}, bf16[5632,1024]{1,0:T...) while((s32[]{:T(128)}, ...), condition=%wide.region_4.5_spmd.clone, body=%wide.region_1.4_spmd.clone.sunk | while | flops 2263448064 | bytes 59939468 | solution.py:50
  218.8 0.6 dynamic_slice.56
  222.0 0.6 broadcast_compare_fusion.2
  222.7 9.3 %fusion.51 = (f32[192,4]{0,1:T(4,128)S(1)}, f32[192,4,5632]{2,0,1:T(8,128)}) fusion(pred[192,5632]{1,0:T(8,128)(4,1)S(1)} %broadcast_compare_fusion.2, bf16[5632,1024]{1,0:T(8,128)(2,1)} %get-tuple-element.212, s32[]{:T(128)S(6)} %select_n.94, bf16[1,192,4,128]{3,2,0,1:T(4,128)(2,1)S(1)} %constant_dynamic-slice_fusion.2), kind=kOutput, calls=%fused_computation.5.clone.1 | convolution fusion | flops 1120271616 | bytes 20024324 | tf_op jit(solution)/shard_map/while/body/eval_jaxpr/qhd,kd->qhk/dot_general | solution.py:15
  232.0 10.3 %fusion.52 = f32[192,4]{0,1:T(4,128)S(1)} fusion(f32[192,4,5632]{2,0,1:T(8,128)} %get-tuple-element.178, f32[192,4]{0,1:T(4,128)S(1)} %get-tuple-element.179, pred[192,5632]{1,0:T(8,128)(4,1)S(1)} %broadcast_compare_fusion.2), kind=kLoop, calls=%fused_computation.6.clone.1 | loop fusion | flops 17300736 | bytes 18388992 | tf_op jit(solution)/shard_map/while/body/eval_jaxpr/reduce_sum | solution.py:41
  242.3 9.2 %fusion.53 = bf16[8,192,4,128]{3,1,2,0:T(8,128)(2,1)} fusion(bf16[8,192,4,128]{3,1,2,0:T(8,128)(2,1)} %get-tuple-element.195, s32[]{:T(128)} %get-tuple-element.194, bf16[5632,1024]{1,0:T(8,128)(2,1)} %get-tuple-element.212, s32[]{:T(128)S(6)} %select_n.93, f32[192,4,5632]{2,0,1:T(8,128)} %get-tuple-element.178, ...), kind=kOutput, calls=%fused_computation.19.clone.1 | convolution fusion | flops 1124794368 | bytes 20027908 | tf_op jit(solution)/shard_map/while/body/eval_jaxpr/qhk,kd->qhd/dot_general | solution.py:44
  254.7 0.6 broadcast_compare_fusion.2
  255.4 9.3 %fusion.51 = (f32[192,4]{0,1:T(4,128)S(1)}, f32[192,4,5632]{2,0,1:T(8,128)}) fusion(pred[192,5632]{1,0:T(8,128)(4,1)S(1)} %broadcast_compare_fusion.2, bf16[5632,1024]{1,0:T(8,128)(2,1)} %get-tuple-element.212, s32[]{:T(128)S(6)} %select_n.94, bf16[1,192,4,128]{3,2,0,1:T(4,128)(2,1)S(1)} %constant_dynamic-slice_fusion.2), kind=kOutput, calls=%fused_computation.5.clone.1 | convolution fusion | flops 1120271616 | bytes 20024324 | tf_op jit(solution)/shard_map/while/body/eval_jaxpr/qhd,kd->qhk/dot_general | solution.py:15
  264.7 10.3 %fusion.52 = f32[192,4]{0,1:T(4,128)S(1)} fusion(f32[192,4,5632]{2,0,1:T(8,128)} %get-tuple-element.178, f32[192,4]{0,1:T(4,128)S(1)} %get-tuple-element.179, pred[192,5632]{1,0:T(8,128)(4,1)S(1)} %broadcast_compare_fusion.2), kind=kLoop, calls=%fused_computation.6.clone.1 | loop fusion | flops 17300736 | bytes 18388992 | tf_op jit(solution)/shard_map/while/body/eval_jaxpr/reduce_sum | solution.py:41
  275.0 9.2 %fusion.53 = bf16[8,192,4,128]{3,1,2,0:T(8,128)(2,1)} fusion(bf16[8,192,4,128]{3,1,2,0:T(8,128)(2,1)} %get-tuple-element.195, s32[]{:T(128)} %get-tuple-element.194, bf16[5632,1024]{1,0:T(8,128)(2,1)} %get-tuple-element.212, s32[]{:T(128)S(6)} %select_n.93, f32[192,4,5632]{2,0,1:T(8,128)} %get-tuple-element.178, ...), kind=kOutput, calls=%fused_computation.19.clone.1 | convolution fusion | flops 1124794368 | bytes 20027908 | tf_op jit(solution)/shard_map/while/body/eval_jaxpr/qhk,kd->qhd/dot_general | solution.py:44
  287.3 0.6 broadcast_compare_fusion.2
  288.1 9.3 %fusion.51 = (f32[192,4]{0,1:T(4,128)S(1)}, f32[192,4,5632]{2,0,1:T(8,128)}) fusion(pred[192,5632]{1,0:T(8,128)(4,1)S(1)} %broadcast_compare_fusion.2, bf16[5632,1024]{1,0:T(8,128)(2,1)} %get-tuple-element.212, s32[]{:T(128)S(6)} %select_n.94, bf16[1,192,4,128]{3,2,0,1:T(4,128)(2,1)S(1)} %constant_dynamic-slice_fusion.2), kind=kOutput, calls=%fused_computation.5.clone.1 | convolution fusion | flops 1120271616 | bytes 20024324 | tf_op jit(solution)/shard_map/while/body/eval_jaxpr/qhd,kd->qhk/dot_general | solution.py:15
  297.3 10.3 %fusion.52 = f32[192,4]{0,1:T(4,128)S(1)} fusion(f32[192,4,5632]{2,0,1:T(8,128)} %get-tuple-element.178, f32[192,4]{0,1:T(4,128)S(1)} %get-tuple-element.179, pred[192,5632]{1,0:T(8,128)(4,1)S(1)} %broadcast_compare_fusion.2), kind=kLoop, calls=%fused_computation.6.clone.1 | loop fusion | flops 17300736 | bytes 18388992 | tf_op jit(solution)/shard_map/while/body/eval_jaxpr/reduce_sum | solution.py:41
  307.7 9.2 %fusion.53 = bf16[8,192,4,128]{3,1,2,0:T(8,128)(2,1)} fusion(bf16[8,192,4,128]{3,1,2,0:T(8,128)(2,1)} %get-tuple-element.195, s32[]{:T(128)} %get-tuple-element.194, bf16[5632,1024]{1,0:T(8,128)(2,1)} %get-tuple-element.212, s32[]{:T(128)S(6)} %select_n.93, f32[192,4,5632]{2,0,1:T(8,128)} %get-tuple-element.178, ...), kind=kOutput, calls=%fused_computation.19.clone.1 | convolution fusion | flops 1124794368 | bytes 20027908 | tf_op jit(solution)/shard_map/while/body/eval_jaxpr/qhk,kd->qhd/dot_general | solution.py:44
  320.0 0.6 broadcast_compare_fusion.2
  320.7 9.3 %fusion.51 = (f32[192,4]{0,1:T(4,128)S(1)}, f32[192,4,5632]{2,0,1:T(8,128)}) fusion(pred[192,5632]{1,0:T(8,128)(4,1)S(1)} %broadcast_compare_fusion.2, bf16[5632,1024]{1,0:T(8,128)(2,1)} %get-tuple-element.212, s32[]{:T(128)S(6)} %select_n.94, bf16[1,192,4,128]{3,2,0,1:T(4,128)(2,1)S(1)} %constant_dynamic-slice_fusion.2), kind=kOutput, calls=%fused_computation.5.clone.1 | convolution fusion | flops 1120271616 | bytes 20024324 | tf_op jit(solution)/shard_map/while/body/eval_jaxpr/qhd,kd->qhk/dot_general | solution.py:15
  330.0 10.3 %fusion.52 = f32[192,4]{0,1:T(4,128)S(1)} fusion(f32[192,4,5632]{2,0,1:T(8,128)} %get-tuple-element.178, f32[192,4]{0,1:T(4,128)S(1)} %get-tuple-element.179, pred[192,5632]{1,0:T(8,128)(4,1)S(1)} %broadcast_compare_fusion.2), kind=kLoop, calls=%fused_computation.6.clone.1 | loop fusion | flops 17300736 | bytes 18388992 | tf_op jit(solution)/shard_map/while/body/eval_jaxpr/reduce_sum | solution.py:41
  340.4 9.2 %fusion.53 = bf16[8,192,4,128]{3,1,2,0:T(8,128)(2,1)} fusion(bf16[8,192,4,128]{3,1,2,0:T(8,128)(2,1)} %get-tuple-element.195, s32[]{:T(128)} %get-tuple-element.194, bf16[5632,1024]{1,0:T(8,128)(2,1)} %get-tuple-element.212, s32[]{:T(128)S(6)} %select_n.93, f32[192,4,5632]{2,0,1:T(8,128)} %get-tuple-element.178, ...), kind=kOutput, calls=%fused_computation.19.clone.1 | convolution fusion | flops 1124794368 | bytes 20027908 | tf_op jit(solution)/shard_map/while/body/eval_jaxpr/qhk,kd->qhd/dot_general | solution.py:44
  352.7 0.6 broadcast_compare_fusion.2
  353.4 9.3 %fusion.51 = (f32[192,4]{0,1:T(4,128)S(1)}, f32[192,4,5632]{2,0,1:T(8,128)}) fusion(pred[192,5632]{1,0:T(8,128)(4,1)S(1)} %broadcast_compare_fusion.2, bf16[5632,1024]{1,0:T(8,128)(2,1)} %get-tuple-element.212, s32[]{:T(128)S(6)} %select_n.94, bf16[1,192,4,128]{3,2,0,1:T(4,128)(2,1)S(1)} %constant_dynamic-slice_fusion.2), kind=kOutput, calls=%fused_computation.5.clone.1 | convolution fusion | flops 1120271616 | bytes 20024324 | tf_op jit(solution)/shard_map/while/body/eval_jaxpr/qhd,kd->qhk/dot_general | solution.py:15
  362.7 10.3 %fusion.52 = f32[192,4]{0,1:T(4,128)S(1)} fusion(f32[192,4,5632]{2,0,1:T(8,128)} %get-tuple-element.178, f32[192,4]{0,1:T(4,128)S(1)} %get-tuple-element.179, pred[192,5632]{1,0:T(8,128)(4,1)S(1)} %broadcast_compare_fusion.2), kind=kLoop, calls=%fused_computation.6.clone.1 | loop fusion | flops 17300736 | bytes 18388992 | tf_op jit(solution)/shard_map/while/body/eval_jaxpr/reduce_sum | solution.py:41
  373.1 9.2 %fusion.53 = bf16[8,192,4,128]{3,1,2,0:T(8,128)(2,1)} fusion(bf16[8,192,4,128]{3,1,2,0:T(8,128)(2,1)} %get-tuple-element.195, s32[]{:T(128)} %get-tuple-element.194, bf16[5632,1024]{1,0:T(8,128)(2,1)} %get-tuple-element.212, s32[]{:T(128)S(6)} %select_n.93, f32[192,4,5632]{2,0,1:T(8,128)} %get-tuple-element.178, ...), kind=kOutput, calls=%fused_computation.19.clone.1 | convolution fusion | flops 1124794368 | bytes 20027908 | tf_op jit(solution)/shard_map/while/body/eval_jaxpr/qhk,kd->qhd/dot_general | solution.py:44
  385.4 0.6 broadcast_compare_fusion.2
  386.1 9.3 %fusion.51 = (f32[192,4]{0,1:T(4,128)S(1)}, f32[192,4,5632]{2,0,1:T(8,128)}) fusion(pred[192,5632]{1,0:T(8,128)(4,1)S(1)} %broadcast_compare_fusion.2, bf16[5632,1024]{1,0:T(8,128)(2,1)} %get-tuple-element.212, s32[]{:T(128)S(6)} %select_n.94, bf16[1,192,4,128]{3,2,0,1:T(4,128)(2,1)S(1)} %constant_dynamic-slice_fusion.2), kind=kOutput, calls=%fused_computation.5.clone.1 | convolution fusion | flops 1120271616 | bytes 20024324 | tf_op jit(solution)/shard_map/while/body/eval_jaxpr/qhd,kd->qhk/dot_general | solution.py:15
  395.4 10.3 %fusion.52 = f32[192,4]{0,1:T(4,128)S(1)} fusion(f32[192,4,5632]{2,0,1:T(8,128)} %get-tuple-element.178, f32[192,4]{0,1:T(4,128)S(1)} %get-tuple-element.179, pred[192,5632]{1,0:T(8,128)(4,1)S(1)} %broadcast_compare_fusion.2), kind=kLoop, calls=%fused_computation.6.clone.1 | loop fusion | flops 17300736 | bytes 18388992 | tf_op jit(solution)/shard_map/while/body/eval_jaxpr/reduce_sum | solution.py:41
  405.7 9.2 %fusion.53 = bf16[8,192,4,128]{3,1,2,0:T(8,128)(2,1)} fusion(bf16[8,192,4,128]{3,1,2,0:T(8,128)(2,1)} %get-tuple-element.195, s32[]{:T(128)} %get-tuple-element.194, bf16[5632,1024]{1,0:T(8,128)(2,1)} %get-tuple-element.212, s32[]{:T(128)S(6)} %select_n.93, f32[192,4,5632]{2,0,1:T(8,128)} %get-tuple-element.178, ...), kind=kOutput, calls=%fused_computation.19.clone.1 | convolution fusion | flops 1124794368 | bytes 20027908 | tf_op jit(solution)/shard_map/while/body/eval_jaxpr/qhk,kd->qhd/dot_general | solution.py:44
  418.1 0.6 broadcast_compare_fusion.2
  418.8 9.3 %fusion.51 = (f32[192,4]{0,1:T(4,128)S(1)}, f32[192,4,5632]{2,0,1:T(8,128)}) fusion(pred[192,5632]{1,0:T(8,128)(4,1)S(1)} %broadcast_compare_fusion.2, bf16[5632,1024]{1,0:T(8,128)(2,1)} %get-tuple-element.212, s32[]{:T(128)S(6)} %select_n.94, bf16[1,192,4,128]{3,2,0,1:T(4,128)(2,1)S(1)} %constant_dynamic-slice_fusion.2), kind=kOutput, calls=%fused_computation.5.clone.1 | convolution fusion | flops 1120271616 | bytes 20024324 | tf_op jit(solution)/shard_map/while/body/eval_jaxpr/qhd,kd->qhk/dot_general | solution.py:15
  428.1 10.3 %fusion.52 = f32[192,4]{0,1:T(4,128)S(1)} fusion(f32[192,4,5632]{2,0,1:T(8,128)} %get-tuple-element.178, f32[192,4]{0,1:T(4,128)S(1)} %get-tuple-element.179, pred[192,5632]{1,0:T(8,128)(4,1)S(1)} %broadcast_compare_fusion.2), kind=kLoop, calls=%fused_computation.6.clone.1 | loop fusion | flops 17300736 | bytes 18388992 | tf_op jit(solution)/shard_map/while/body/eval_jaxpr/reduce_sum | solution.py:41
  438.4 9.2 %fusion.53 = bf16[8,192,4,128]{3,1,2,0:T(8,128)(2,1)} fusion(bf16[8,192,4,128]{3,1,2,0:T(8,128)(2,1)} %get-tuple-element.195, s32[]{:T(128)} %get-tuple-element.194, bf16[5632,1024]{1,0:T(8,128)(2,1)} %get-tuple-element.212, s32[]{:T(128)S(6)} %select_n.93, f32[192,4,5632]{2,0,1:T(8,128)} %get-tuple-element.178, ...), kind=kOutput, calls=%fused_computation.19.clone.1 | convolution fusion | flops 1124794368 | bytes 20027908 | tf_op jit(solution)/shard_map/while/body/eval_jaxpr/qhk,kd->qhd/dot_general | solution.py:44
  450.7 0.6 broadcast_compare_fusion.2
  451.5 9.3 %fusion.51 = (f32[192,4]{0,1:T(4,128)S(1)}, f32[192,4,5632]{2,0,1:T(8,128)}) fusion(pred[192,5632]{1,0:T(8,128)(4,1)S(1)} %broadcast_compare_fusion.2, bf16[5632,1024]{1,0:T(8,128)(2,1)} %get-tuple-element.212, s32[]{:T(128)S(6)} %select_n.94, bf16[1,192,4,128]{3,2,0,1:T(4,128)(2,1)S(1)} %constant_dynamic-slice_fusion.2), kind=kOutput, calls=%fused_computation.5.clone.1 | convolution fusion | flops 1120271616 | bytes 20024324 | tf_op jit(solution)/shard_map/while/body/eval_jaxpr/qhd,kd->qhk/dot_general | solution.py:15
  460.8 10.3 %fusion.52 = f32[192,4]{0,1:T(4,128)S(1)} fusion(f32[192,4,5632]{2,0,1:T(8,128)} %get-tuple-element.178, f32[192,4]{0,1:T(4,128)S(1)} %get-tuple-element.179, pred[192,5632]{1,0:T(8,128)(4,1)S(1)} %broadcast_compare_fusion.2), kind=kLoop, calls=%fused_computation.6.clone.1 | loop fusion | flops 17300736 | bytes 18388992 | tf_op jit(solution)/shard_map/while/body/eval_jaxpr/reduce_sum | solution.py:41
  471.1 9.2 %fusion.53 = bf16[8,192,4,128]{3,1,2,0:T(8,128)(2,1)} fusion(bf16[8,192,4,128]{3,1,2,0:T(8,128)(2,1)} %get-tuple-element.195, s32[]{:T(128)} %get-tuple-element.194, bf16[5632,1024]{1,0:T(8,128)(2,1)} %get-tuple-element.212, s32[]{:T(128)S(6)} %select_n.93, f32[192,4,5632]{2,0,1:T(8,128)} %get-tuple-element.178, ...), kind=kOutput, calls=%fused_computation.19.clone.1 | convolution fusion | flops 1124794368 | bytes 20027908 | tf_op jit(solution)/shard_map/while/body/eval_jaxpr/qhk,kd->qhd/dot_general | solution.py:44
  480.2 2.7 copy.15
  483.0 2.4 broadcast_in_dim_reshape.3
  (32 shorter events, 5.0 us)
Async XLA Ops:
  6.5 124.1 %copy-start = (bf16[1,8,77,1024]{3,1,2,0:T(8,128)(2,1)S(1)}, bf16[1,8,77,1024]{3,1,2,0:T(8,128)(2,1)}, u32[]{:S(2)}) copy-start(bf16[1,8,77,1024]{3,1,2,0:T(8,128)(2,1)} %param.13) | copy-start | bytes 3784708
  6.5 117.7 %all-gather.5.cloned.1.call-start = ((), (), s32[]{:S(2)}) async-start(), calls=%async_computation | async-start | bytes 17825792 | tf_op jit(solution)/shard_map/all_gather | solution.py:61
  7.3 146.4 %all-gather.9.cloned.1.call-start = ((), (), s32[]{:S(2)}) async-start(), calls=%async_computation.2 | async-start | bytes 3538944 | tf_op jit(solution)/shard_map/all_gather | solution.py:78
  8.0 197.1 %all-gather.7.cloned.1.call-start = ((), (), s32[]{:S(2)}) async-start(), calls=%async_computation.1 | async-start | bytes 9437184 | tf_op jit(solution)/shard_map/all_gather | solution.py:77
  205.1 13.7 %copy-start.2 = (s32[5632]{0:T(1024)S(1)}, s32[5632]{0:T(1024)}, u32[]{:S(2)}) copy-start(s32[5632]{0:T(1024)} %constant.95.clone.1) | copy-start | bytes 67588
  480.2 5.1 %copy-start.1 = (bf16[1,8,77,1024]{3,1,2,0:T(8,128)(2,1)S(1)}, bf16[1,8,77,1024]{3,1,2,0:T(8,128)(2,1)}, u32[]{:S(2)}) copy-start(bf16[1,8,77,1024]{3,1,2,0:T(8,128)(2,1)} %param.13) | copy-start | bytes 3784708
Sparse Core Ops, SparseCore 0:
  9.5 114.6 all-gather.4
  125.9 27.7 all-gather.8
  155.4 49.7 all-gather.6
where the time goes:
time: 493 us; the launch traced here: 492 us
  waiting for transfers between devices  183 us (37%)
  matrix products  151 us (31%)
  other arithmetic  103 us (21%)
  local copies, waits for them, and re-layouts  21.1 us (4%)
  loops' own time  20.7 us (4%)
  between operations  13.2 us (3%)
    all_gather x1, waiting for transfers between devices, on_device(): gathered = lax.all_gather(kv_store, 'cache', axis=0, tiled=True)  113 us
    reduce_sum x8, other arithmetic, one_block(): totals = jnp.sum(weights, axis=-1)  82.7 us
    dot_general x8, matrix products, block_scores(): jnp.einsum('qhd,kd->qhk', query_block, key_block, preferred_element_type=...  74.3 us
    dot_general x8, matrix products, one_block(): jnp.einsum('qhk,kd->qhd', rounded, value_block, preferred_element_type=jn...  73.3 us
    all_gather x1, waiting for transfers between devices, on_device(): lax.all_gather(context, 'seq', axis=1, tiled=True)  51.5 us
    another operation x1, loops' own time, attend_rows(): lax.map(one_block, (jnp.arange(block_count, dtype=jnp.int32), query_block...  20.7 us
    all_gather x1, waiting for transfers between devices, on_device(): lax.all_gather(own_question, 'seq', axis=0, tiled=True)  16.9 us
    concatenate x1, other arithmetic, on_device(): jnp.concatenate([full_context.reshape(context_count, features), full_ques...  13.7 us
  transfers between devices with their start and end apart: 3, of which 3 were waited for; matrix products, arithmetic and copies ran while one was open for 3% of the time, Pallas kernels for 0%

commit v1 on v0

v1 whole, which is shorter than its diff:
```python
import functools

import jax
import jax.numpy as jnp
from jax import lax
from jax.experimental import pallas as pl
from jax.experimental.pallas import tpu as pltpu
from jax.sharding import PartitionSpec as P

HD = 128
KVH = 4
GROUP = 8
SPANS = 8
MOST = 2
SLOTS_DEV = 8
PARTS = 2
RB = 512
LOG2E = 1.4426950408889634
SCALE = LOG2E * HD**-0.5
MASKED = -1.0e30
MESH = pl.DeviceIdType.MESH


def kernel(
    nc, ns,
    span_slot, retrieval, recompute, fresh_hbm, queries_hbm, question_hbm, store_hbm,
    out_hbm,
    *scratch,
):
    steps = KVH * PARTS
    recv = scratch[:steps]
    (send, store, fresh, query, out, ctx, ques, fresh_rows, keep, qt, acc, peak, vt, scores,
     slot_row, slot_all, slot_smem, send_slot, own_slot,
     local_sem, route_send, route_recv, route_smem, a2a_send, a2a_recv, ring_out, ring_in) = scratch[steps:]
    c = lax.axis_index("cache")
    s = lax.axis_index("seq")
    x, core = s // 2, s % 2
    right = lax.rem(x + 1, 4) * 2 + core
    left = lax.rem(x + 3, 4) * 2 + core
    far = lax.rem(x + 2, 4) * 2 + core
    sibling = x * 2 + (1 - core)
    tokens = store.shape[1]
    part = tokens // PARTS
    qlen = query.shape[0]
    rows = GROUP * qlen
    units = rows // RB

    def local(i):
        src, dst = (
            (store_hbm, store),
            (question_hbm.at[0], ques.at[s]),
            (queries_hbm.at[0], query),
            (fresh_hbm.at[0], fresh),
        )[i]
        return pltpu.make_async_copy(src, dst, local_sem.at[i])

    for i in range(4):
        local(i).start()

    lane = lax.broadcasted_iota(jnp.int32, (8, 128), 1)
    row = jnp.zeros((8, 128), jnp.int32)
    own = [span_slot[retrieval[0, j]] for j in range(SPANS)]
    for j in range(SPANS):
        row = jnp.where(lane == j, own[j], row)
        owner = own[j] // SLOTS_DEV
        rank = jnp.int32(0)
        for k in range(j):
            rank = rank + (own[k] // SLOTS_DEV == owner).astype(jnp.int32)
        own_slot[0, j] = owner
        own_slot[1, j] = jnp.minimum(rank, MOST - 1)
    slot_row[...] = row
    slot_all[c] = row

    barrier = pltpu.get_barrier_semaphore()

    def greet(d, _):
        pl.semaphore_signal(barrier, inc=1, device_id=(lax.rem(c + d, nc), s), device_id_type=MESH)
        return 0

    lax.fori_loop(1, nc, greet, 0)
    for peer in (left, right, sibling):
        pl.semaphore_signal(barrier, inc=1, device_id=(c, peer), device_id_type=MESH)
    pl.semaphore_wait(barrier, nc + 2)

    def route_copy(d):
        return pltpu.make_async_remote_copy(
            src_ref=slot_row, dst_ref=slot_all.at[c], send_sem=route_send.at[d], recv_sem=route_recv.at[d],
            device_id=(lax.rem(c + d, nc), s), device_id_type=MESH)

    def route_start(d, _):
        route_copy(d).start()
        return 0

    lax.fori_loop(1, nc, route_start, 0)

    def ring_copy(buf, b, n, source, peer, lo=None):
        at = buf.at[source]
        if lo is not None:
            half = buf.shape[1] // 2
            at = at.at[pl.ds(lo * half, half)]
        return pltpu.make_async_remote_copy(
            src_ref=at, dst_ref=at, send_sem=ring_out.at[b, n], recv_sem=ring_in.at[b, n],
            device_id=(c, peer), device_id_type=MESH)

    def other(index):
        return index // 2 * 2 + (1 - core)

    def ring_send(buf, b, n):
        source, peer, lo = (
            (s, right, None), (s, left, None), (s, sibling, None), (left, right, 0),
            (left, sibling, None), (right, left, 1), (right, sibling, None), (far, sibling, None),
        )[n]
        return ring_copy(buf, b, n, source, peer, lo)

    def ring_arrive(buf, b, n):
        source, peer, lo = (
            (left, right, None), (right, left, None), (other(s), sibling, None), (far, right, 0),
            (other(left), sibling, None), (far, left, 1), (other(right), sibling, None), (other(far), sibling, None),
        )[n]
        ring_copy(buf, b, n, source, peer, lo).wait_recv()

    def ring_first(buf, b):
        for n in (0, 1, 2):
            ring_send(buf, b, n).start()

    def ring_second(buf, b):
        for arrival, onward in ((0, (3, 4)), (1, (5, 6))):
            ring_arrive(buf, b, arrival)
            for n in onward:
                ring_send(buf, b, n).start()

    def ring_third(buf, b):
        ring_arrive(buf, b, 3)
        ring_arrive(buf, b, 5)
        ring_send(buf, b, 7).start()

    def ring_last(buf, b):
        for n in (2, 4, 6, 7):
            ring_arrive(buf, b, n)

    def ring_sent(buf, b):
        for n in range(8):
            ring_send(buf, b, n).wait_send()

    local(1).wait()
    ring_first(ques, steps)

    def route_wait(d, _):
        pltpu.make_async_remote_copy(
            src_ref=slot_row, dst_ref=slot_all.at[lax.rem(c + nc - d, nc)], send_sem=route_send.at[d],
            recv_sem=route_recv.at[d], device_id=(lax.rem(c + d, nc), s), device_id_type=MESH).wait()
        return 0

    lax.fori_loop(1, nc, route_wait, 0)
    to_smem = pltpu.make_async_copy(slot_all.at[:, 0], slot_smem, route_smem)
    to_smem.start()
    to_smem.wait()

    def route(r, _):
        count, first, second = jnp.int32(0), jnp.int32(0), jnp.int32(0)
        for j in range(SPANS):
            slot = slot_smem[r, j]
            mine = slot // SLOTS_DEV == c
            at = slot % SLOTS_DEV
            first = jnp.where(jnp.logical_and(mine, count == 0), at, first)
            second = jnp.where(jnp.logical_and(mine, count == 1), at, second)
            count = count + mine.astype(jnp.int32)
        send_slot[r, 0] = first
        send_slot[r, 1] = second
        return 0

    lax.fori_loop(0, nc, route, 0)
    local(0).wait()

    def fill(i):
        h, t = i // PARTS, i % PARTS

        def one(r, _):
            for k in range(MOST):
                at = send_slot[r, k]
                send[i, r, k, :, :HD] = store[at, t * part:(t + 1) * part, h * HD:(h + 1) * HD]
                send[i, r, k, :, HD:] = store[at, t * part:(t + 1) * part, (KVH + h) * HD:(KVH + h + 1) * HD]
            return 0

        lax.fori_loop(0, nc, one, 0)
        recv[i][c] = send[i, c]

        def start(d, _):
            to = lax.rem(c + d, nc)
            pltpu.make_async_remote_copy(
                src_ref=send.at[i, to], dst_ref=recv[i].at[c], send_sem=a2a_send.at[i], recv_sem=a2a_recv.at[i],
                device_id=(to, s), device_id_type=MESH).start()
            return 0

        lax.fori_loop(1, nc, start, 0)

    for i in range(steps):
        fill(i)

    local(3).wait()
    place = s * tokens + lax.broadcasted_iota(jnp.int32, (tokens, recompute.shape[2]), 0)
    for j in range(SPANS):
        hit = recompute[0, j:j + 1, :] == place
        picked = jnp.where(hit, 1.0, 0.0)
        fresh_rows[j] = jnp.dot(
            picked.astype(jnp.bfloat16), fresh[j], preferred_element_type=jnp.float32
        ).astype(jnp.bfloat16)
        kept = 1.0 - jnp.sum(picked, axis=1, keepdims=True)
        keep[j] = jnp.broadcast_to(kept, (tokens, HD)).astype(jnp.bfloat16)

    ring_second(ques, steps)

    local(2).wait()
    for h in range(KVH * GROUP):
        g, j = h // GROUP, h % GROUP
        qt[g, :, j * qlen:(j + 1) * qlen] = query[:, h * HD:(h + 1) * HD].astype(jnp.float32).T.astype(jnp.bfloat16)
    acc[...] = jnp.zeros_like(acc)
    peak[...] = jnp.full_like(peak, MASKED)
    vt[HD:] = jnp.ones_like(vt[HD:])
    ring_third(ques, steps)

    def choose(i):
        h, t = i // PARTS, i % PARTS
        pltpu.make_async_copy(recv[i].at[pl.ds(0, nc - 1)], recv[i].at[pl.ds(0, nc - 1)], a2a_recv.at[i]).wait()
        for j in range(SPANS):
            got = recv[i][own_slot[0, j], own_slot[1, j]]
            kept = keep[j, t * part:(t + 1) * part, :]
            fill_k = fresh_rows[j, t * part:(t + 1) * part, h * HD:(h + 1) * HD]
            fill_v = fresh_rows[j, t * part:(t + 1) * part, (KVH + h) * HD:(KVH + h + 1) * HD]
            ctx[i, s, j * part:(j + 1) * part, :HD] = got[:, :HD] * kept + fill_k
            ctx[i, s, j * part:(j + 1) * part, HD:] = got[:, HD:] * kept + fill_v
        ring_first(ctx.at[i], i)

    def attend(g, keys, values, hidden, hooks):
        count = keys.shape[0]
        vt[:HD, :count] = values.T

        def fill_scores(u):
            scores[u % 2, :count] = jnp.dot(
                keys, qt[g, :, u * RB:(u + 1) * RB], preferred_element_type=jnp.float32)

        fill_scores(0)
        for u in range(units):
            if u < len(hooks):
                hooks[u]()
            if u + 1 < units:
                fill_scores(u + 1)
            cols = slice(u * RB, (u + 1) * RB)
            score = scores[u % 2, :count]
            if hidden is not None:
                score = hidden(score, u)
            old = peak[g, :, cols]
            new = jnp.maximum(old, jnp.max(score, axis=0, keepdims=True))
            peak[g, :, cols] = new
            weight = jnp.exp2((score - new) * SCALE).astype(jnp.bfloat16)
            shrink = jnp.exp2((old - new) * SCALE)
            add = jnp.dot(vt[:, :count], weight, preferred_element_type=jnp.float32)
            acc[g, :, cols] = acc[g, :, cols] * shrink + add[:acc.shape[1]]

    ring_last(ques, steps)

    half = ns // 2

    def question_step(n, _):
        g, b = n // 2, n % 2

        @pl.when(b * half <= s)
        def _():
            block = ques.at[pl.ds(b * half, half)]
            keys = block[:, :, pl.ds(pl.multiple_of(g * HD, HD), HD)].reshape(half * qlen, HD)
            values = block[:, :, pl.ds(pl.multiple_of((KVH + g) * HD, HD), HD)].reshape(half * qlen, HD)

            def hidden(score, u):
                key_at = b * half * qlen + lax.broadcasted_iota(jnp.int32, score.shape, 0)
                col = u * RB + lax.broadcasted_iota(jnp.int32, score.shape, 1)
                return jnp.where(key_at <= s * qlen + col % qlen, score, MASKED)

            attend(g, keys, values, hidden, ())

        @pl.when(n == 2)
        def _():
            choose(0)

        @pl.when(n == 4)
        def _():
            ring_second(ctx.at[0], 0)

        @pl.when(n == 6)
        def _():
            ring_third(ctx.at[0], 0)

        return 0

    lax.fori_loop(0, 2 * KVH, question_step, 0)
    ring_last(ctx.at[0], 0)

    def context_step(i, _):
        g = i // PARTS

        def hook_first():
            for k in range(1, steps):
                @pl.when(i + 1 == k)
                def _():
                    choose(k)

        def hook_second():
            @pl.when(i + 1 < steps)
            def _():
                ring_second(ctx.at[i + 1], i + 1)

        def hook_third():
            @pl.when(i + 1 < steps)
            def _():
                ring_third(ctx.at[i + 1], i + 1)

        block = ctx.at[i]
        count = ns * SPANS * part
        keys = block[:, :, :HD].reshape(count, HD)
        values = block[:, :, HD:].reshape(count, HD)
        attend(g, keys, values, None, (hook_first, hook_second, hook_third))

        @pl.when(i % PARTS == PARTS - 1)
        def _():
            for j in range(GROUP):
                cols = slice(j * qlen, (j + 1) * qlen)
                o = acc[g, :HD, cols] / acc[g, HD:HD + 1, cols]
                out[g, :, j * HD:(j + 1) * HD] = o.T.astype(out.dtype)
            out_copy(g).start()

        @pl.when(i + 1 < steps)
        def _():
            ring_last(ctx.at[i + 1], i + 1)

        return 0

    def out_copy(g):
        return pltpu.make_async_copy(
            out.at[g], out_hbm.at[0, :, pl.ds(pl.multiple_of(g * GROUP * HD, HD), GROUP * HD)], local_sem.at[4 + g])

    lax.fori_loop(0, steps, context_step, 0)

    ring_sent(ques, steps)

    def sent(i, _):
        ring_sent(ctx.at[i], i)
        pltpu.make_async_copy(send.at[i, pl.ds(0, nc - 1)], send.at[i, pl.ds(0, nc - 1)], a2a_send.at[i]).wait()
        return 0

    lax.fori_loop(0, steps, sent, 0)
    for g in range(KVH):
        out_copy(g).wait()


def on_device(nc, ns, kv_store, span_slot, retrieval, recompute, fresh_kv, queries, question_kv):
    slots, tokens, features = kv_store.shape
    qlen = queries.shape[1]
    rows = GROUP * qlen
    steps = KVH * PARTS
    part = tokens // PARTS
    recomp = recompute.shape[2]
    bf16, f32, i32 = jnp.bfloat16, jnp.float32, jnp.int32
    dma = pltpu.SemaphoreType.DMA
    any_space = pl.BlockSpec(memory_space=pl.ANY)
    smem = pl.BlockSpec(memory_space=pltpu.SMEM)
    vmem = pl.BlockSpec(memory_space=pltpu.VMEM)
    keys = ns * SPANS * part
    scratch = [pltpu.VMEM((nc, MOST, part, 2 * HD), bf16) for _ in range(steps)] + [
        pltpu.VMEM((steps, nc, MOST, part, 2 * HD), bf16),
        pltpu.VMEM((slots, tokens, features), bf16),
        pltpu.VMEM((SPANS, recomp, features), bf16),
        pltpu.VMEM((qlen, KVH * GROUP * HD), bf16),
        pltpu.VMEM((KVH, qlen, GROUP * HD), bf16),
        pltpu.VMEM((steps, ns, SPANS * part, 2 * HD), bf16),
        pltpu.VMEM((ns, qlen, features), bf16),
        pltpu.VMEM((SPANS, tokens, features), bf16),
        pltpu.VMEM((SPANS, tokens, HD), bf16),
        pltpu.VMEM((KVH, HD, rows), bf16),
        pltpu.VMEM((KVH, HD + 8, rows), f32),
        pltpu.VMEM((KVH, 1, rows), f32),
        pltpu.VMEM((HD + 16, keys), bf16),
        pltpu.VMEM((2, keys, RB), f32),
        pltpu.VMEM((8, 128), i32),
        pltpu.VMEM((nc, 8, 128), i32),
        pltpu.SMEM((nc, 128), i32),
        pltpu.SMEM((nc, MOST), i32),
        pltpu.SMEM((2, SPANS), i32),
        dma((8,)),
        dma((nc,)),
        dma((nc,)),
        dma,
        dma((steps,)),
        dma((steps,)),
        dma((steps + 1, 8)),
        dma((steps + 1, 8)),
    ]
    return pl.pallas_call(
        functools.partial(kernel, nc, ns),
        out_shape=jax.ShapeDtypeStruct(queries.shape, queries.dtype),
        in_specs=[smem, smem, vmem, any_space, any_space, any_space, any_space],
        out_specs=any_space,
        scratch_shapes=scratch,
        compiler_params=pltpu.CompilerParams(
            collective_id=0, has_side_effects=True, vmem_limit_bytes=60 * 2**20
        ),
        name="spans_attention",
    )(span_slot, retrieval, recompute, fresh_kv, queries, question_kv, kv_store)


def solution(mesh):
    in_specs = (
        P("cache", "seq", None),
        P(),
        P("cache", None),
        P("cache", None, None),
        P("cache", None, None, None),
        P("cache", "seq", None),
        P("cache", "seq", None),
    )
    out_specs = P("cache", "seq", None)
    return jax.shard_map(
        functools.partial(on_device, mesh.shape["cache"], mesh.shape["seq"]),
        mesh=mesh, in_specs=in_specs, out_specs=out_specs, check_vma=False,
    )
```

time: 493 us -> 135 us (0.27)
  waiting for transfers between devices: 183 us -> 0 us
  matrix products: 151 us -> 0 us
  Pallas kernels: 0 us -> 129 us
  other arithmetic: 103 us -> 0 us
  loops' own time: 20.7 us -> 0 us
  local copies, waits for them, and re-layouts: 21.1 us -> 5.75 us
  between operations: 13.2 us -> 0.01 us
    all_gather x3 -> x0, waiting for transfers between devices: 182 us -> none  [the longest x1 113 us: on_device(): gathered = lax.all_gather(kv_store, 'cache', axis=0, tiled=True)]
    dot_general x17 -> x0, matrix products: 151 us -> none  [the longest x8 74.3 us: block_scores(): jnp.einsum('qhd,kd->qhk', query_block, key_block, preferred_element_type=...]
    pallas_call x0 -> x1, Pallas kernels: none -> 129 us  [on_device(): pl.pallas_call(functools.partial(kernel, nc, ns), out_shape=jax.ShapeDtyp...]
    reduce_sum x8 -> x0, other arithmetic: 82.7 us -> none  [one_block(): totals = jnp.sum(weights, axis=-1)]
    another operation x1 -> x0, loops' own time: 20.7 us -> none  [attend_rows(): lax.map(one_block, (jnp.arange(block_count, dtype=jnp.int32), query_block...]
    concatenate x1 -> x0, other arithmetic: 13.7 us -> none  [on_device(): jnp.concatenate([full_context.reshape(context_count, features), full_ques...]
    gather x2 -> x0, local copies, waits for them, and re-layouts: 7.68 us -> none  [the longest x1 6.38 us: on_device(): cached = gathered[own_slots]]
    unnamed x6 -> x2, local copies, waits for them, and re-layouts: 0.01 us -> 5.75 us
  transfers between devices with their start and end apart: 3 -> 0, of which waited for: 3 -> 0; matrix products, arithmetic and copies ran while one was open for 3% -> 0% of each run, Pallas kernels for 0% -> 0%
where the time goes in v1:
time: 135 us
  Pallas kernels  129 us (96%)
  local copies, waits for them, and re-layouts  5.75 us (4%)
    pallas_call x1, Pallas kernels, on_device(): pl.pallas_call(functools.partial(kernel, nc, ns), out_shape=jax.ShapeDtyp...  129 us
    unnamed x2, local copies, waits for them, and re-layouts  5.75 us

profile of v1, /device:TPU:1, one launch (start us, length us, event | category | flops | bytes accessed | tf_op | source)
XLA Modules:
  0.0 134.6 jit_solution(11732377705529985096)
XLA Ops:
  0.0 3.0 %copy.8.fresh_hbm = bf16[1,8,77,1024]{3,2,1,0:T(8,128)(2,1)} copy(bf16[1,8,77,1024]{3,1,2,0:T(8,128)(2,1)} %param.11) | data formatting | bytes 2523136 | tf_op args[4]
  3.0 128.9 %spans_attention.1 = bf16[1,192,4096]{2,1,0:T(8,128)(2,1)} custom-call(s32[128]{0:T(128)} %span_slot.1, s32[1,8]{1,0:T(1,128)} %retrieval.1, s32[1,8,77]{2,1,0:T(8,128)} %recompute.1, bf16[1,8,77,1024]{3,2,1,0:T(8,128)(2,1)} %copy.8.fresh_hbm, bf16[1,192,4096]{2,1,0:T(8,128)(2,1)} %queries_hbm.1, bf16[1,192,1024]{2,1,0:T(8,128)(2,1)} %question_hbm.1, ...), custom_call_target="tpu_custom_call" | custom-call | tf_op jit(solution)/shard_map/spans_attention/pallas_call | solution.py:396
  131.9 2.7 %copy.10 = bf16[1,192,4096]{2,1,0:T(8,128)(2,1)} copy(bf16[1,192,4096]{2,1,0:T(8,128)(2,1)} %spans_attention.1) | data formatting | bytes 3145728

commit v2 on v1

v2 whole, which is shorter than its diff:
```python
import functools

import jax
import jax.numpy as jnp
from jax import lax
from jax.experimental import pallas as pl
from jax.experimental.pallas import tpu as pltpu
from jax.sharding import PartitionSpec as P

HD = 128
KVH = 4
GROUP = 8
SPANS = 8
MOST = 2
SLOTS_DEV = 8
SLOT_BITS = 3
PARTS = 4
RB = 512
AHEAD = (14,8,2)
QUESTION_PACE = (4,7)
LOG2E = 1.4426950408889634
SCALE = LOG2E * HD**-0.5
MASKED = -1.0e30
MESH = pl.DeviceIdType.MESH


def kernel(
    nc, ns,
    span_slot, retrieval, recompute, fresh_hbm, queries_hbm, question_hbm, store_hbm,
    out_hbm,
    *scratch,
):
    steps = KVH * PARTS
    recv = scratch[:steps]
    (send, store, fresh, query, out, ctx, ques, onehot, fresh_rows, keep, qt, acc, peak, vt, scores,
     slot_row, slot_all, slot_smem, own_slot,
     local_sem, route_send, route_recv, route_smem, a2a_send, a2a_recv, ring_out, ring_in) = scratch[steps:]
    c = lax.axis_index("cache")
    s = lax.axis_index("seq")
    x, core = s // 2, s % 2

    def peer_at(me, d):
        return (me + d) & (nc - 1)

    right = lax.rem(x + 1, 4) * 2 + core
    left = lax.rem(x + 3, 4) * 2 + core
    far = lax.rem(x + 2, 4) * 2 + core
    sibling = x * 2 + (1 - core)
    tokens = store.shape[1]
    part = tokens // PARTS
    qlen = query.shape[0]
    rows = GROUP * qlen
    units = rows // RB

    barrier = pltpu.get_barrier_semaphore()
    for d in range(1, nc):
        pl.semaphore_signal(barrier, inc=1, device_id=(peer_at(c, d), s), device_id_type=MESH)
    for peer in (left, right, sibling):
        pl.semaphore_signal(barrier, inc=1, device_id=(c, peer), device_id_type=MESH)

    def local(i):
        if i < 2 * KVH:
            g, half = i // 2, i % 2
            src = question_hbm.at[0, :, pl.ds((half * KVH + g) * HD, HD)]
            dst = ques.at[g, s, :, pl.ds(half * HD, HD)]
        else:
            src, dst = ((store_hbm, store), (queries_hbm.at[0], query), (fresh_hbm, fresh))[i - 2 * KVH]
        return pltpu.make_async_copy(src, dst, local_sem.at[i])

    for i in range(2 * KVH + 3):
        local(i).start()

    lane = lax.broadcasted_iota(jnp.int32, (8, 128), 1)
    wanted = jnp.zeros((8, 128), jnp.int32)
    own = [span_slot[retrieval[0, j]] for j in range(SPANS)]
    owners = [lax.shift_right_logical(slot, SLOT_BITS) for slot in own]
    for j in range(SPANS):
        rank = jnp.int32(0)
        for k in range(j):
            rank = rank + (owners[k] == owners[j]).astype(jnp.int32)
        rank = jnp.minimum(rank, MOST - 1)
        wanted = jnp.where(lane == owners[j] + nc * rank, own[j] & (SLOTS_DEV - 1), wanted)
        own_slot[0, j] = owners[j]
        own_slot[1, j] = rank
    slot_row[...] = wanted
    slot_all[c] = wanted
    pl.semaphore_wait(barrier, nc + 2)

    def route_copy(d, at):
        return pltpu.make_async_remote_copy(
            src_ref=slot_row.at[0], dst_ref=slot_all.at[at, 0], send_sem=route_send.at[d], recv_sem=route_recv.at[d],
            device_id=(peer_at(c, d), s), device_id_type=MESH)

    for d in range(1, nc):
        route_copy(d, c).start()

    def ring_copy(buf, b, n, source, peer, lo=None):
        at = buf.at[source]
        if lo is not None:
            half = buf.shape[1] // 2
            at = at.at[pl.ds(lo * half, half)]
        return pltpu.make_async_remote_copy(
            src_ref=at, dst_ref=at, send_sem=ring_out.at[b, n], recv_sem=ring_in.at[b, n],
            device_id=(c, peer), device_id_type=MESH)

    def other(index):
        return index // 2 * 2 + (1 - core)

    def ring_send(buf, b, n):
        source, peer, lo = (
            (s, right, None), (s, left, None), (s, sibling, None), (left, right, 0),
            (left, sibling, None), (right, left, 1), (right, sibling, None), (far, sibling, None),
        )[n]
        return ring_copy(buf, b, n, source, peer, lo)

    def ring_arrive(buf, b, n):
        source, peer, lo = (
            (left, right, None), (right, left, None), (other(s), sibling, None), (far, right, 0),
            (other(left), sibling, None), (far, left, 1), (other(right), sibling, None), (other(far), sibling, None),
        )[n]
        ring_copy(buf, b, n, source, peer, lo).wait_recv()

    def ring_first(buf, b):
        for n in (0, 1, 2):
            ring_send(buf, b, n).start()

    def ring_second(buf, b):
        for arrival, onward in ((0, (3, 4)), (1, (5, 6))):
            ring_arrive(buf, b, arrival)
            for n in onward:
                ring_send(buf, b, n).start()

    def ring_third(buf, b):
        ring_arrive(buf, b, 3)
        ring_arrive(buf, b, 5)
        ring_send(buf, b, 7).start()

    def ring_last(buf, b):
        for n in (2, 4, 6, 7):
            ring_arrive(buf, b, n)

    def ring_sent(buf, b):
        for n in range(8):
            ring_send(buf, b, n).wait_send()

    for g in range(KVH):
        local(2 * g).wait()
        local(2 * g + 1).wait()
        ring_first(ques.at[g], steps + g)

    local(2 * KVH + 1).wait()
    for h in range(KVH * GROUP):
        g, j = h // GROUP, h % GROUP
        qt[g, :, j * qlen:(j + 1) * qlen] = query[:, h * HD:(h + 1) * HD].astype(jnp.float32).T.astype(jnp.bfloat16)

    local(2 * KVH + 2).wait()
    count = fresh.shape[0]
    place = recompute[0]
    spread = (
        lax.broadcasted_iota(jnp.int32, (place.shape[1], count), 1) // SPANS
        == lax.broadcasted_iota(jnp.int32, (place.shape[1], count), 0)
    ).astype(jnp.float32).astype(jnp.bfloat16)

    def spread_out(values):
        return jnp.dot(values.astype(jnp.float32).astype(jnp.bfloat16), spread, preferred_element_type=jnp.float32)

    places = spread_out(place // 16) * 16.0 + spread_out(place % 16)
    token = (s * tokens + lax.broadcasted_iota(jnp.int32, (tokens, count), 0)).astype(jnp.float32)
    span = lax.broadcasted_iota(jnp.int32, (tokens, count), 1) % SPANS
    for j in range(SPANS):
        hit = jnp.logical_and(places[j:j + 1, :] == token, span == j)
        picked = jnp.where(hit, 1.0, 0.0)
        onehot[j * tokens:(j + 1) * tokens, :] = picked.astype(jnp.bfloat16)
        kept = 1.0 - jnp.sum(picked, axis=1, keepdims=True)
        keep[j] = jnp.broadcast_to(kept, (tokens, HD)).astype(jnp.bfloat16)
    fresh_rows[...] = jnp.dot(onehot[...], fresh[...], preferred_element_type=jnp.float32).astype(
        jnp.bfloat16).reshape(fresh_rows.shape)

    acc[...] = jnp.zeros_like(acc)
    peak[...] = jnp.full_like(peak, MASKED)
    vt[HD:] = jnp.ones_like(vt[HD:])

    for d in range(1, nc):
        route_copy(d, peer_at(c, nc - d)).wait()
    to_smem = pltpu.make_async_copy(slot_all.at[:, 0], slot_smem, route_smem)
    to_smem.start()
    local(2 * KVH).wait()
    to_smem.wait()

    def fill(i):
        h, t = i // PARTS, i % PARTS

        def one(r, _):
            for k in range(MOST):
                at = slot_smem[r, c + nc * k]
                send[i, r, k, :, :HD] = store[at, t * part:(t + 1) * part, h * HD:(h + 1) * HD]
                send[i, r, k, :, HD:] = store[at, t * part:(t + 1) * part, (KVH + h) * HD:(KVH + h + 1) * HD]
            return 0

        lax.fori_loop(0, nc, one, 0)
        recv[i][c] = send[i, c]

        def start(d, _):
            to = peer_at(c, d)
            pltpu.make_async_remote_copy(
                src_ref=send.at[i, to], dst_ref=recv[i].at[c], send_sem=a2a_send.at[i], recv_sem=a2a_recv.at[i],
                device_id=(to, s), device_id_type=MESH).start()
            return 0

        lax.fori_loop(1, nc, start, 0)

    for i in range(steps):
        fill(i)

    def choose(i):
        h, t = i // PARTS, i % PARTS
        pltpu.make_async_copy(recv[i].at[pl.ds(0, nc - 1)], recv[i].at[pl.ds(0, nc - 1)], a2a_recv.at[i]).wait()
        for j in range(SPANS):
            got = recv[i][own_slot[0, j], own_slot[1, j]]
            kept = keep[j, t * part:(t + 1) * part, :]
            fill_k = fresh_rows[j, t * part:(t + 1) * part, h * HD:(h + 1) * HD]
            fill_v = fresh_rows[j, t * part:(t + 1) * part, (KVH + h) * HD:(KVH + h + 1) * HD]
            ctx[i, s, j * part:(j + 1) * part, :HD] = got[:, :HD] * kept + fill_k
            ctx[i, s, j * part:(j + 1) * part, HD:] = got[:, HD:] * kept + fill_v
        ring_first(ctx.at[i], i)

    def attend(g, keys, values, hidden, hook):
        count = keys.shape[0]
        vt[:HD, :count] = values.T

        def fill_scores(u):
            scores[u % 2, :count] = jnp.dot(
                keys, qt[g, :, u * RB:(u + 1) * RB], preferred_element_type=jnp.float32)

        fill_scores(0)
        for u in range(units):
            if hook is not None:
                hook(u)
            if u + 1 < units:
                fill_scores(u + 1)
            cols = slice(u * RB, (u + 1) * RB)
            score = scores[u % 2, :count]
            if hidden is not None:
                score = hidden(score, u)
            old = peak[g, :, cols]
            new = jnp.maximum(old, jnp.max(score, axis=0, keepdims=True))
            peak[g, :, cols] = new
            weight = jnp.exp2((score - new) * SCALE).astype(jnp.bfloat16)
            shrink = jnp.exp2((old - new) * SCALE)
            add = jnp.dot(vt[:, :count], weight, preferred_element_type=jnp.float32)
            acc[g, :, cols] = acc[g, :, cols] * shrink + add[:acc.shape[1]]

    half = ns // 2

    def second(k):
        ring_second(ctx.at[k], k)

    def third(k):
        ring_third(ctx.at[k], k)

    def question_second(g):
        ring_second(ques.at[g], steps + g)

    def question_third(g):
        ring_third(ques.at[g], steps + g)

    question_second(0)
    question_second(1)
    question_third(0)
    question_second(2)

    stages = ((third, AHEAD[2]), (second, AHEAD[1]), (choose, AHEAD[0]))
    prologue = [(0, question_third, 1), (0, question_second, 3), (2, question_third, 2), (4, question_third, 3)]
    for slot in range(-AHEAD[0], 0):
        for stage, ahead in stages:
            k = (slot + ahead) // units
            if (slot + ahead) % units == 0 and 0 <= k < steps:
                prologue.append((max(0, 2 * KVH + slot * QUESTION_PACE[0] // QUESTION_PACE[1]), stage, k))

    def question_step(n, _):
        g, b = n // 2, n % 2

        @pl.when(b == 0)
        def _():
            ring_last(ques.at[g], steps + g)

        @pl.when(b * half <= s)
        def _():
            block = ques.at[g, pl.ds(b * half, half)]
            keys = block[:, :, :HD].reshape(half * qlen, HD)
            values = block[:, :, HD:].reshape(half * qlen, HD)

            def hidden(score, u):
                key_at = b * half * qlen + lax.broadcasted_iota(jnp.int32, score.shape, 0)
                col = u * RB + lax.broadcasted_iota(jnp.int32, score.shape, 1)
                return jnp.where(key_at <= s * qlen + col % qlen, score, MASKED)

            attend(g, keys, values, hidden, None)

        for at, stage, k in prologue:
            @pl.when(n == at)
            def _():
                stage(k)

        return 0

    lax.fori_loop(0, 2 * KVH, question_step, 0)
    ring_last(ctx.at[0], 0)

    def context_step(i, _):
        g = i // PARTS

        def hook(u):
            for stage, ahead in stages:
                if (u + ahead) % units == 0:
                    later = (u + ahead) // units
                    if stage is choose:
                        for k in range(later, steps):
                            @pl.when(i + later == k)
                            def _():
                                choose(k)
                    else:
                        @pl.when(i + later < steps)
                        def _():
                            stage(i + later)

        block = ctx.at[i]
        count = ns * SPANS * part
        keys = block[:, :, :HD].reshape(count, HD)
        values = block[:, :, HD:].reshape(count, HD)
        attend(g, keys, values, None, hook)

        @pl.when(i % PARTS == PARTS - 1)
        def _():
            for j in range(GROUP):
                cols = slice(j * qlen, (j + 1) * qlen)
                o = acc[g, :HD, cols] / acc[g, HD:HD + 1, cols]
                out[g, :, j * HD:(j + 1) * HD] = o.T.astype(out.dtype)
            out_copy(g).start()

        @pl.when(i + 1 < steps)
        def _():
            ring_last(ctx.at[i + 1], i + 1)

        return 0

    def out_copy(g):
        return pltpu.make_async_copy(
            out.at[g], out_hbm.at[0, :, pl.ds(pl.multiple_of(g * GROUP * HD, HD), GROUP * HD)], local_sem.at[2 * KVH + 3 + g])

    lax.fori_loop(0, steps, context_step, 0)

    for g in range(KVH):
        ring_sent(ques.at[g], steps + g)

    def sent(i, _):
        ring_sent(ctx.at[i], i)
        pltpu.make_async_copy(send.at[i, pl.ds(0, nc - 1)], send.at[i, pl.ds(0, nc - 1)], a2a_send.at[i]).wait()
        return 0

    lax.fori_loop(0, steps, sent, 0)
    for g in range(KVH):
        out_copy(g).wait()


def on_device(nc, ns, kv_store, span_slot, retrieval, recompute, fresh_kv, queries, question_kv):
    slots, tokens, features = kv_store.shape
    qlen = queries.shape[1]
    rows = GROUP * qlen
    steps = KVH * PARTS
    part = tokens // PARTS
    recomp = recompute.shape[2]
    bf16, f32, i32 = jnp.bfloat16, jnp.float32, jnp.int32
    dma = pltpu.SemaphoreType.DMA
    any_space = pl.BlockSpec(memory_space=pl.ANY)
    smem = pl.BlockSpec(memory_space=pltpu.SMEM)
    vmem = pl.BlockSpec(memory_space=pltpu.VMEM)
    keys = ns * SPANS * part
    scratch = [pltpu.VMEM((nc, MOST, part, 2 * HD), bf16) for _ in range(steps)] + [
        pltpu.VMEM((steps, nc, MOST, part, 2 * HD), bf16),
        pltpu.VMEM((slots, tokens, features), bf16),
        pltpu.VMEM((SPANS * recomp, features), bf16),
        pltpu.VMEM((qlen, KVH * GROUP * HD), bf16),
        pltpu.VMEM((KVH, qlen, GROUP * HD), bf16),
        pltpu.VMEM((steps, ns, SPANS * part, 2 * HD), bf16),
        pltpu.VMEM((KVH, ns, qlen, 2 * HD), bf16),
        pltpu.VMEM((SPANS * tokens, SPANS * recomp), bf16),
        pltpu.VMEM((SPANS, tokens, features), bf16),
        pltpu.VMEM((SPANS, tokens, HD), bf16),
        pltpu.VMEM((KVH, HD, rows), bf16),
        pltpu.VMEM((KVH, HD + 8, rows), f32),
        pltpu.VMEM((KVH, 1, rows), f32),
        pltpu.VMEM((HD + 16, keys), bf16),
        pltpu.VMEM((2, keys, RB), f32),
        pltpu.VMEM((8, 128), i32),
        pltpu.VMEM((nc, 8, 128), i32),
        pltpu.SMEM((nc, 128), i32),
        pltpu.SMEM((2, SPANS), i32),
        dma((3 * KVH + 3,)),
        dma((nc,)),
        dma((nc,)),
        dma,
        dma((steps,)),
        dma((steps,)),
        dma((steps + KVH, 8)),
        dma((steps + KVH, 8)),
    ]
    return pl.pallas_call(
        functools.partial(kernel, nc, ns),
        out_shape=jax.ShapeDtypeStruct(queries.shape, queries.dtype),
        in_specs=[smem, smem, vmem, any_space, any_space, any_space, any_space],
        out_specs=any_space,
        scratch_shapes=scratch,
        compiler_params=pltpu.CompilerParams(
            collective_id=0, has_side_effects=True, vmem_limit_bytes=60 * 2**20
        ),
        name="spans_attention",
    )(span_slot, retrieval, recompute, fresh_kv[0].transpose(1, 0, 2).reshape(SPANS * recomp, features), queries, question_kv, kv_store)


def solution(mesh):
    in_specs = (
        P("cache", "seq", None),
        P(),
        P("cache", None),
        P("cache", None, None),
        P("cache", None, None, None),
        P("cache", "seq", None),
        P("cache", "seq", None),
    )
    out_specs = P("cache", "seq", None)
    return jax.shard_map(
        functools.partial(on_device, mesh.shape["cache"], mesh.shape["seq"]),
        mesh=mesh, in_specs=in_specs, out_specs=out_specs, check_vma=False,
    )
```

time: 135 us -> 82 us (0.61)
  Pallas kernels: 129 us -> 79.2 us
  local copies, waits for them, and re-layouts: 5.75 us -> 2.7 us
    pallas_call x1, Pallas kernels: 129 us -> 79.2 us  [on_device(): pl.pallas_call(functools.partial(kernel, nc, ns), out_shape=jax.ShapeDtyp...]
    unnamed x2 -> x1, local copies, waits for them, and re-layouts: 5.75 us -> 2.7 us
where the time goes in v2:
time: 82 us; the launch traced here: 81.9 us
  Pallas kernels  79.2 us (97%)
  local copies, waits for them, and re-layouts  2.7 us (3%)
    pallas_call x1, Pallas kernels, on_device(): pl.pallas_call(functools.partial(kernel, nc, ns), out_shape=jax.ShapeDtyp...  79.2 us
    unnamed x1, local copies, waits for them, and re-layouts  2.7 us

profile of v2, /device:TPU:1, one launch (start us, length us, event | category | flops | bytes accessed | tf_op | source)
XLA Modules:
  0.0 81.9 jit_solution(13104953948068218770)
XLA Ops:
  0.0 79.2 %spans_attention.1 = bf16[1,192,4096]{2,1,0:T(8,128)(2,1)} custom-call(s32[128]{0:T(128)} %span_slot.1, s32[1,8]{1,0:T(1,128)} %retrieval.1, s32[1,8,77]{2,1,0:T(8,128)} %recompute.1, bf16[616,1024]{1,0:T(8,128)(2,1)} %bitcast.5, bf16[1,192,4096]{2,1,0:T(8,128)(2,1)} %queries_hbm.1, bf16[1,192,1024]{2,1,0:T(8,128)(2,1)} %question_hbm.1, ...), custom_call_target="tpu_custom_call" | custom-call | tf_op jit(solution)/shard_map/spans_attention/pallas_call | solution.py:408
  79.2 2.7 %copy.9 = bf16[1,192,4096]{2,1,0:T(8,128)(2,1)} copy(bf16[1,192,4096]{2,1,0:T(8,128)(2,1)} %spans_attention.1) | data formatting | bytes 3145728
